TPU v7x, 32 devices: a whole 2x2x4 slice. The times are simulated.
32 devices in a mesh: row: 8 (over z, y), col: 4 (over x, core).
Axes of the slice: x: 2, y: 2, z: 4, core: 2. Of those that a mesh axis runs over, the one named last changes fastest.
Arguments:
- features: float32 [16384, 512], P(('row', 'col')), may hold values from -6 to 6
- tiles: float32 [8, 4, 128, 128, 128], P('row', 'col'), may hold values from -0.4 to 0.4
- tile_rows: int32 [8, 4, 128], P('row', 'col'), may hold values from 0 to 15
- tile_cols: int32 [8, 4, 128], P('row', 'col'), may hold values from 0 to 15
- tile_count: int32 [8, 4], P('row', 'col'), may hold values from 16 to 128, as said below
- needed: int32 [8, 4, 8, 2], P('row', 'col'), may hold values from 0 to 3, as said below
- w_in: bfloat16 [512, 2048], replicated, may hold values from -0.25 to 0.25
- bias_in: float32 [2048], replicated, may hold values from -5 to 5
- w_out: bfloat16 [2048, 512], replicated, may hold values from -0.125 to 0.125
- bias_out: float32 [512], replicated, may hold values from -5 to 5
Outputs:
- updated: bfloat16 [16384, 512], P(('row', 'col'))
Inputs may be any that keep to these rules, and one draw needn't show every extreme that they name: tile_count of every grid cell lies between 16 and 64, except one cell of each draw that has all 128 tiles live. Each list needed[r, c, q] holds 2 different block numbers.
All inputs are finite; a program needn't handle non-finite values.
Results may differ from a plain program's by a relative error of at most 0.0054.
Values sent between devices are 32-bit elements; how exact they have to be, the bound alone decides.
A program may use at most 128 MiB of HBM per device.

v0:
```python
import math

import jax
import jax.numpy as jnp
from jax import lax
from jax.sharding import PartitionSpec as P

gin_epsilon = 0.25
precise_mode = lax.Precision.HIGHEST


def on_device(
    features, tiles, tile_rows, tile_cols, tile_count, needed, w_in, bias_in, w_out, bias_out
):
    tile_edge = tiles.shape[-1]
    width = features.shape[1]
    blocks_dev = features.shape[0] // tile_edge
    grid_rows = lax.axis_size("row")
    grid_cols = lax.axis_size("col")
    slot_count = needed.shape[-1]
    own_blocks = features.reshape(blocks_dev, tile_edge, width)
    my_tiles = tiles[0, 0]
    tile_row = tile_rows[0, 0]
    tile_col = tile_cols[0, 0]
    wanted = needed[0, 0]
    requests = lax.all_to_all(wanted, "row", split_axis=0, concat_axis=0, tiled=True)
    chosen = jnp.take(own_blocks, requests.reshape(-1), axis=0).reshape(
        grid_rows, slot_count, tile_edge, width
    )
    received = lax.all_to_all(chosen, "row", split_axis=0, concat_axis=0, tiled=True)
    column_pool = received.reshape(grid_rows * slot_count, tile_edge, width)
    tile_total = my_tiles.shape[0]
    group = math.gcd(32, tile_total)
    row_blocks = grid_cols * blocks_dev
    live = (jnp.arange(tile_total) < tile_count[0, 0]).astype(jnp.float32)
    block_ids = jnp.arange(row_blocks, dtype=jnp.int32)

    def add_group(turn, partial_value):
        start = turn * group
        group_tiles = lax.dynamic_slice_in_dim(my_tiles, start, group, 0)
        group_pos = lax.dynamic_slice_in_dim(tile_col, start, group, 0)
        group_row = lax.dynamic_slice_in_dim(tile_row, start, group, 0)
        group_live = lax.dynamic_slice_in_dim(live, start, group, 0)
        inputs = jnp.take(column_pool, group_pos, axis=0)
        product = jnp.einsum("tpq,tqf->tpf", group_tiles, inputs, precision=precise_mode)
        selector = (group_row[None, :] == block_ids[:, None]).astype(jnp.float32) * group_live[
            None, :
        ]
        return partial_value + jnp.dot(
            selector, product.reshape(group, tile_edge * width), precision=precise_mode
        )

    partial_value = lax.fori_loop(
        0, tile_total // group, add_group, jnp.zeros((row_blocks, tile_edge * width), jnp.float32)
    )
    summed = lax.psum_scatter(
        partial_value.reshape(row_blocks * tile_edge, width), "col", scatter_dimension=0, tiled=True
    )
    mixed = ((1.0 + gin_epsilon) * features + summed).astype(jnp.bfloat16)
    hidden = jax.nn.relu(jnp.dot(mixed, w_in, preferred_element_type=jnp.float32) + bias_in).astype(
        jnp.bfloat16
    )
    return (jnp.dot(hidden, w_out, preferred_element_type=jnp.float32) + bias_out).astype(
        jnp.bfloat16
    )


def solution(mesh):
    placed = (
        P(("row", "col"), None),
        P("row", "col", None, None, None),
        P("row", "col", None),
        P("row", "col", None),
        P("row", "col"),
        P("row", "col", None, None),
        P(),
        P(),
        P(),
        P(),
    )
    return jax.shard_map(
        on_device, mesh=mesh, in_specs=placed, out_specs=P(("row", "col"), None), check_vma=False
    )
```

profile of v0, /device:TPU:0, one launch (start us, length us, event | category | flops | bytes accessed | tf_op | source)
XLA Modules:
  0.0 324.2 jit_solution(2764501017054242542)
XLA Ops:
  7.4 13.5 %all_to_all.14 = s32[8,1,2]{2,1,0:T(1,128)S(1)} all-to-all(s32[8,1,2]{2,1,0:T(1,128)S(1)} %copy.15), channel_id=1, replica_groups=mesh['row'=8,'col'=4] {'row'}, dimensions={0} | all-to-all | bytes 128 | tf_op jit(solution)/shard_map/all_to_all | solution.py:26
  22.4 4.0 %gather_fusion.1 = f32[16,128,512]{2,1,0:T(8,128)} fusion(f32[4,128,512]{2,1,0:T(8,128)} %bitcast.27, s32[1024]{0:T(1024)S(1)} %pad_clamp_fusion.1), kind=kCustom, calls=%fused_computation.1 | custom fusion | bytes 8388672 | tf_op jit(solution)/shard_map/jit(_take)/gather | solution.py:27
  26.5 4.9 %broadcast_select_fusion = f32[8,2,128,512]{3,2,1,0:T(8,128)} fusion(f32[8,2,128,512]{3,2,1,0:T(8,128)} %bitcast.26, pred[8,2]{1,0:T(8,128)(4,1)S(1)} %copy.17), kind=kLoop, calls=%fused_computation.21 | loop fusion | flops 1048576 | bytes 8388624 | tf_op jit(solution)/shard_map/jit(_take)/select_n | solution.py:27
  31.4 4.7 %all-to-all-start.1 = ((f32[8,2,128,512]{3,2,1,0:T(8,128)}), f32[8,2,128,512]{3,2,1,0:T(8,128)}, u32[]{:S(2)}, u32[]{:S(2)}) async-start(f32[8,2,128,512]{3,2,1,0:T(8,128)} %broadcast_select_fusion), calls=%async_computation.1 | async-start | bytes 8388608 | tf_op jit(solution)/shard_map/all_to_all | solution.py:30
  36.8 91.3 %all-to-all-done.1 = f32[8,2,128,512]{3,2,1,0:T(8,128)} async-done(((f32[8,2,128,512]{3,2,1,0:T(8,128)}), f32[8,2,128,512]{3,2,1,0:T(8,128)}, u32[]{:S(2)}, u32[]{:S(2)}) %all-to-all-start.1) | async-done | bytes 4194336 | tf_op jit(solution)/shard_map/all_to_all | solution.py:30
  128.1 136.5 %while.14 = (s32[]{:T(128)}, f32[16,65536]{1,0:T(8,128)}, s32[128]{0:T(128)S(1)}, f32[128]{0:T(128)S(1)}, f32[128,128,128]{2,1,0:T(8,128)}, /*index=5*/s32[128]{...) while((s32[]{:T(128)}, f32[16,65536]{1,0:T(8,128)}, ...), condition=%wide.region_1.2_spmd.clone, body=%wide.region_0.1_spmd.clone.sunk | while | flops 3628075264 | bytes 69211632 | solution.py:53
  128.2 6.5 %gather_fusion = f32[32,128,512]{2,1,0:T(8,128)} fusion(f32[16,128,512]{2,1,0:T(8,128)} %get-tuple-element.262, s32[1024]{0:T(1024)S(1)} %pad_clamp_fusion.3), kind=kCustom, calls=%fused_computation.clone.clone.1 | custom fusion | bytes 16777344 | tf_op jit(solution)/shard_map/while/body/eval_jaxpr/jit(_take)/gather | solution.py:44
  134.7 10.9 %fusion.33 = f32[32,128,512]{2,1,0:T(8,128)S(1)} fusion(f32[32,128,512]{2,1,0:T(8,128)} %gather_fusion, pred[32]{0:T(512)(128)(4,1)S(1)} %get-tuple-element.233, f32[128,128,128]{2,1,0:T(8,128)} %get-tuple-element.260, s32[]{:T(128)S(6)} %select_n.69), kind=kOutput, calls=%fused_computation.4.clone.1 | convolution fusion | flops 3223322624 | bytes 18874404 | tf_op jit(solution)/shard_map/while/body/eval_jaxpr/tpq,tqf->tpf/dot_general | solution.py:45
  145.6 8.1 %copy.20 = f32[4,8,128,512]{3,1,2,0:T(8,128)} copy(f32[4,8,128,512]{3,2,1,0:T(8,128)S(1)} %bitcast.25) | data formatting | bytes 16777216 | tf_op jit(solution)/shard_map/while
  153.9 7.9 %convolution_add_fusion.3 = f32[16,65536]{1,0:T(8,128)} fusion(f32[32,65536]{1,0:T(8,128)} %bitcast.24, f32[16,65536]{1,0:T(8,128)} %get-tuple-element.246, pred[]{:T(512)S(6)} %compare.3, f32[32]{0:T(128)S(1)} %dynamic_slice.40, s32[32]{0:T(128)S(1)} %dynamic_slice.41), kind=kOutput, calls=%fused_computation.3.clone.1 | convolution fusion | flops 404751360 | bytes 16777472 | tf_op jit(solution)/shard_map/while/body/eval_jaxpr/dot_general | solution.py:49
  161.8 6.5 %gather_fusion = f32[32,128,512]{2,1,0:T(8,128)} fusion(f32[16,128,512]{2,1,0:T(8,128)} %get-tuple-element.262, s32[1024]{0:T(1024)S(1)} %pad_clamp_fusion.3), kind=kCustom, calls=%fused_computation.clone.clone.1 | custom fusion | bytes 16777344 | tf_op jit(solution)/shard_map/while/body/eval_jaxpr/jit(_take)/gather | solution.py:44
  168.3 10.9 %fusion.33 = f32[32,128,512]{2,1,0:T(8,128)S(1)} fusion(f32[32,128,512]{2,1,0:T(8,128)} %gather_fusion, pred[32]{0:T(512)(128)(4,1)S(1)} %get-tuple-element.233, f32[128,128,128]{2,1,0:T(8,128)} %get-tuple-element.260, s32[]{:T(128)S(6)} %select_n.69), kind=kOutput, calls=%fused_computation.4.clone.1 | convolution fusion | flops 3223322624 | bytes 18874404 | tf_op jit(solution)/shard_map/while/body/eval_jaxpr/tpq,tqf->tpf/dot_general | solution.py:45
  179.2 8.1 %copy.20 = f32[4,8,128,512]{3,1,2,0:T(8,128)} copy(f32[4,8,128,512]{3,2,1,0:T(8,128)S(1)} %bitcast.25) | data formatting | bytes 16777216 | tf_op jit(solution)/shard_map/while
  187.5 8.5 %convolution_add_fusion.3 = f32[16,65536]{1,0:T(8,128)} fusion(f32[32,65536]{1,0:T(8,128)} %bitcast.24, f32[16,65536]{1,0:T(8,128)} %get-tuple-element.246, pred[]{:T(512)S(6)} %compare.3, f32[32]{0:T(128)S(1)} %dynamic_slice.40, s32[32]{0:T(128)S(1)} %dynamic_slice.41), kind=kOutput, calls=%fused_computation.3.clone.1 | convolution fusion | flops 404751360 | bytes 16777472 | tf_op jit(solution)/shard_map/while/body/eval_jaxpr/dot_general | solution.py:49
  196.1 6.5 %gather_fusion = f32[32,128,512]{2,1,0:T(8,128)} fusion(f32[16,128,512]{2,1,0:T(8,128)} %get-tuple-element.262, s32[1024]{0:T(1024)S(1)} %pad_clamp_fusion.3), kind=kCustom, calls=%fused_computation.clone.clone.1 | custom fusion | bytes 16777344 | tf_op jit(solution)/shard_map/while/body/eval_jaxpr/jit(_take)/gather | solution.py:44
  202.6 10.9 %fusion.33 = f32[32,128,512]{2,1,0:T(8,128)S(1)} fusion(f32[32,128,512]{2,1,0:T(8,128)} %gather_fusion, pred[32]{0:T(512)(128)(4,1)S(1)} %get-tuple-element.233, f32[128,128,128]{2,1,0:T(8,128)} %get-tuple-element.260, s32[]{:T(128)S(6)} %select_n.69), kind=kOutput, calls=%fused_computation.4.clone.1 | convolution fusion | flops 3223322624 | bytes 18874404 | tf_op jit(solution)/shard_map/while/body/eval_jaxpr/tpq,tqf->tpf/dot_general | solution.py:45
  213.5 8.1 %copy.20 = f32[4,8,128,512]{3,1,2,0:T(8,128)} copy(f32[4,8,128,512]{3,2,1,0:T(8,128)S(1)} %bitcast.25) | data formatting | bytes 16777216 | tf_op jit(solution)/shard_map/while
  221.8 8.5 %convolution_add_fusion.3 = f32[16,65536]{1,0:T(8,128)} fusion(f32[32,65536]{1,0:T(8,128)} %bitcast.24, f32[16,65536]{1,0:T(8,128)} %get-tuple-element.246, pred[]{:T(512)S(6)} %compare.3, f32[32]{0:T(128)S(1)} %dynamic_slice.40, s32[32]{0:T(128)S(1)} %dynamic_slice.41), kind=kOutput, calls=%fused_computation.3.clone.1 | convolution fusion | flops 404751360 | bytes 16777472 | tf_op jit(solution)/shard_map/while/body/eval_jaxpr/dot_general | solution.py:49
  230.4 6.5 %gather_fusion = f32[32,128,512]{2,1,0:T(8,128)} fusion(f32[16,128,512]{2,1,0:T(8,128)} %get-tuple-element.262, s32[1024]{0:T(1024)S(1)} %pad_clamp_fusion.3), kind=kCustom, calls=%fused_computation.clone.clone.1 | custom fusion | bytes 16777344 | tf_op jit(solution)/shard_map/while/body/eval_jaxpr/jit(_take)/gather | solution.py:44
  236.9 10.9 %fusion.33 = f32[32,128,512]{2,1,0:T(8,128)S(1)} fusion(f32[32,128,512]{2,1,0:T(8,128)} %gather_fusion, pred[32]{0:T(512)(128)(4,1)S(1)} %get-tuple-element.233, f32[128,128,128]{2,1,0:T(8,128)} %get-tuple-element.260, s32[]{:T(128)S(6)} %select_n.69), kind=kOutput, calls=%fused_computation.4.clone.1 | convolution fusion | flops 3223322624 | bytes 18874404 | tf_op jit(solution)/shard_map/while/body/eval_jaxpr/tpq,tqf->tpf/dot_general | solution.py:45
  247.8 8.1 %copy.20 = f32[4,8,128,512]{3,1,2,0:T(8,128)} copy(f32[4,8,128,512]{3,2,1,0:T(8,128)S(1)} %bitcast.25) | data formatting | bytes 16777216 | tf_op jit(solution)/shard_map/while
  256.1 8.5 %convolution_add_fusion.3 = f32[16,65536]{1,0:T(8,128)} fusion(f32[32,65536]{1,0:T(8,128)} %bitcast.24, f32[16,65536]{1,0:T(8,128)} %get-tuple-element.246, pred[]{:T(512)S(6)} %compare.3, f32[32]{0:T(128)S(1)} %dynamic_slice.40, s32[32]{0:T(128)S(1)} %dynamic_slice.41), kind=kOutput, calls=%fused_computation.3.clone.1 | convolution fusion | flops 404751360 | bytes 16777472 | tf_op jit(solution)/shard_map/while/body/eval_jaxpr/dot_general | solution.py:49
  268.5 43.7 %reduce-scatter.2.cloned.1.call-done = f32[512,512]{1,0:T(8,128)} async-done(((f32[2048,512]{1,0:T(8,128)}), f32[512,512]{1,0:T(8,128)}) %reduce-scatter.2.cloned.1.call-update) | async-done | bytes 1048592 | tf_op jit(solution)/shard_map/reduce_scatter | solution.py:56
  312.3 5.1 %fusion.14 = bf16[512,512]{1,0:T(8,128)(2,1)} fusion(bf16[2048,512]{1,0:T(8,128)(2,1)S(1)} %copy-done, bf16[512,2048]{1,0:T(8,128)(2,1)} %param.18, f32[2048]{0:T(1024)S(1)} %copy-done.3, f32[512,512]{1,0:T(8,128)} %reduce-scatter.2.cloned.1.call-done, f32[512,512]{1,0:T(8,128)S(1)} %copy-done.1, f32[512]{0:T(512)S(1)} %copy-done.4), kind=kOutput, calls=%fused_computation.23 | convolution fusion | flops 2151940096 | bytes 6825984 | tf_op jit(solution)/shard_map/dot_general | solution.py:63
  (42 shorter events, 7.3 us)
Async XLA Ops:
  6.5 305.7 %copy-start = (bf16[2048,512]{1,0:T(8,128)(2,1)S(1)}, bf16[2048,512]{1,0:T(8,128)(2,1)}, u32[]{:S(2)}) copy-start(bf16[2048,512]{1,0:T(8,128)(2,1)} %param.20) | copy-start | bytes 6291460
  31.4 96.8 %copy-start.2 = (s32[1,1,128]{2,1,0:T(1,128)S(1)}, s32[1,1,128]{2,1,0:T(1,128)}, u32[]{:S(2)}) copy-start(s32[1,1,128]{2,1,0:T(1,128)} %param.15) | copy-start | bytes 1540
  31.4 96.8 %copy-start.5 = (s32[1,1,128]{2,1,0:T(1,128)S(1)}, s32[1,1,128]{2,1,0:T(1,128)}, u32[]{:S(2)}) copy-start(s32[1,1,128]{2,1,0:T(1,128)} %param.14) | copy-start | bytes 1540
  31.4 96.8 %all-to-all-start.1 = ((f32[8,2,128,512]{3,2,1,0:T(8,128)}), f32[8,2,128,512]{3,2,1,0:T(8,128)}, u32[]{:S(2)}, u32[]{:S(2)}) async-start(f32[8,2,128,512]{3,2,1,0:T(8,128)} %broadcast_select_fusion), calls=%async_computation.1 | async-start | bytes 8388608 | tf_op jit(solution)/shard_map/all_to_all | solution.py:30
  36.1 276.2 %reduce-scatter.2.cloned.1.call-start = ((), (), s32[]{:S(2)}) async-start(), calls=%async_computation.3 | async-start | bytes 5242880 | tf_op jit(solution)/shard_map/reduce_scatter | solution.py:56
  268.5 43.7 %copy-start.1 = (f32[512,512]{1,0:T(8,128)S(1)}, f32[512,512]{1,0:T(8,128)}, u32[]{:S(2)}) copy-start(f32[512,512]{1,0:T(8,128)} %param.12) | copy-start | bytes 3145732
  268.5 43.7 %copy-start.3 = (f32[2048]{0:T(1024)S(1)}, f32[2048]{0:T(1024)}, u32[]{:S(2)}) copy-start(f32[2048]{0:T(1024)} %param.19) | copy-start | bytes 24580
  268.5 43.7 %copy-start.4 = (f32[512]{0:T(512)S(1)}, f32[512]{0:T(512)}, u32[]{:S(2)}) copy-start(f32[512]{0:T(512)} %param.21) | copy-start | bytes 6148
Sparse Core Ops, SparseCore 0:
  268.7 43.5 reduce-scatter.1
where the time goes:
time: 325 us; the launch traced here: 324 us
  waiting for transfers between devices  135 us (42%)
  matrix products  82.1 us (25%)
  local copies, waits for them, and re-layouts  68.6 us (21%)
  between operations  14.1 us (4%)
  blocking collectives  13.5 us (4%)
  other arithmetic  5.92 us (2%)
  starting transfers between devices  4.76 us (1%)
    all_to_all x1, waiting for transfers between devices, on_device(): lax.all_to_all(chosen, 'row', split_axis=0, concat_axis=0, tiled=True)  91.3 us
    reduce_scatter x1, waiting for transfers between devices, on_device(): lax.psum_scatter(partial_value.reshape(row_blocks * tile_edge, width), 'c...  43.7 us
    dot_general x4, matrix products, add_group(): jnp.einsum('tpq,tqf->tpf', group_tiles, inputs, precision=precise_mode)  43.6 us
    dot_general x4, matrix products, add_group(): jnp.dot(selector, product.reshape(group, tile_edge * width), precision=pr...  33.5 us
    while x4, local copies, waits for them, and re-layouts  32.4 us
    gather x4, local copies, waits for them, and re-layouts, add_group(): inputs = jnp.take(column_pool, group_pos, axis=0)  26 us
    all_to_all x1, blocking collectives, on_device(): lax.all_to_all(wanted, 'row', split_axis=0, concat_axis=0, tiled=True)  13.5 us
  transfers between devices with their start and end apart: 2, of which 2 were waited for; matrix products, arithmetic and copies ran while one was open for 0% of the time, Pallas kernels for 0%

commit v1 on v0

v1 whole, which is shorter than its diff:
```python
import functools
import math

import jax
import jax.numpy as jnp
from jax import lax
from jax.experimental import pallas as pl
from jax.experimental.pallas import tpu as pltpu
from jax.sharding import PartitionSpec as P

gin_epsilon = 0.25
MESH = pl.DeviceIdType.MESH
MIB = 1 << 20


def assemble_kernel(rows, cols, count, tiles_ref, out_ref, acc):
    edge = tiles_ref.shape[-1]
    group = acc.shape[0] // edge
    first = pl.program_id(0) * group
    acc[...] = jnp.zeros_like(acc)

    def add(t, carry):
        local = rows[t] - first

        @pl.when((local >= 0) & (local < group))
        def _():
            at_row = pl.multiple_of(local * edge, edge)
            at_col = pl.multiple_of(cols[t] * edge, edge)
            acc[pl.ds(at_row, edge), pl.ds(at_col, edge)] += tiles_ref[t]

        return carry

    lax.fori_loop(0, count[0], add, 0)
    out_ref[...] = acc[...].astype(jnp.bfloat16)


def assemble(tiles, rows, cols, count, targets, slots):
    total, edge, _ = tiles.shape
    groups = max(1, targets * slots * edge * edge * 4 // (8 * MIB))
    height = targets // groups * edge
    return pl.pallas_call(
        assemble_kernel,
        out_shape=jax.ShapeDtypeStruct((targets * edge, slots * edge), jnp.bfloat16),
        grid_spec=pltpu.PrefetchScalarGridSpec(
            num_scalar_prefetch=3,
            grid=(groups,),
            in_specs=[pl.BlockSpec(memory_space=pltpu.VMEM)],
            out_specs=pl.BlockSpec((height, slots * edge), lambda g, *_: (g, 0)),
            scratch_shapes=[pltpu.VMEM((height, slots * edge), jnp.float32)],
        ),
        compiler_params=pltpu.CompilerParams(vmem_limit_bytes=40 * MIB),
        name="assemble",
    )(rows, cols, count, tiles)


def layer_kernel(
    cfg,
    features,
    wanted,
    dense,
    w_in,
    bias_in,
    w_out,
    bias_out,
    out,
    zbuf,
    ysend_buf,
    yrecv_buf,
    asked,
    panels,
    pool,
    partial,
    core_buf,
    x_buf,
    w_in_v,
    w_out_v,
    mixed,
    feat_sem,
    dense_sem,
    w_sem,
    z_recv,
    right_send,
    left_send,
    y_send,
    y_recv,
    ask_send,
    ask_recv,
    core_send,
    core_recv,
    x_send,
    x_recv,
):
    Z, Y, X, J, B, edge, width, chunks, resident = cfg
    owners = 2 * X
    nodes = B * edge
    row, col = lax.axis_index("row"), lax.axis_index("col")
    z, y = row // Y, lax.rem(row, Y)
    x, core = col // 2, lax.rem(col, 2)
    mate = 1 - core

    def turn(base, step, size):
        return lax.rem(base + step + size, size)

    def at_z(other):
        return (other * Y + y, col)

    def at_y(other):
        return (z * Y + other, col)

    def at_x(other, which):
        return (row, other * 2 + which)

    def local_features(k):
        return pltpu.make_async_copy(
            features.at[:, pl.ds(pl.multiple_of(k * width, width), width)],
            zbuf.at[k, z],
            feat_sem.at[k],
        )

    def z_copy(k, source, to, sem):
        return pltpu.make_async_remote_copy(
            src_ref=zbuf.at[k, source],
            dst_ref=zbuf.at[k, source],
            send_sem=sem.at[k, source],
            recv_sem=z_recv.at[k, source],
            device_id=at_z(to),
            device_id_type=MESH,
        )

    def to_right(k, source):
        return z_copy(k, source, z + 1, right_send)

    def to_left(k, source):
        return z_copy(k, source, z - 1, left_send)

    def ask_copy(d):
        return pltpu.make_async_remote_copy(
            src_ref=wanted,
            dst_ref=asked.at[d - 1],
            send_sem=ask_send.at[d - 1],
            recv_sem=ask_recv.at[d - 1],
            device_id=at_y(turn(y, d, Y)),
            device_id_type=MESH,
        )

    def y_copy(k, d, source):
        return pltpu.make_async_remote_copy(
            src_ref=ysend_buf.at[k, d - 1, source],
            dst_ref=yrecv_buf.at[k, d - 1, source],
            send_sem=y_send.at[k, d - 1, source],
            recv_sem=y_recv.at[k, d - 1, source],
            device_id=at_y(turn(y, -d, Y)),
            device_id_type=MESH,
        )

    def core_copy(k, other):
        return pltpu.make_async_remote_copy(
            src_ref=partial.at[k, other * 2 + mate],
            dst_ref=core_buf.at[k, other],
            send_sem=core_send.at[k, other],
            recv_sem=core_recv.at[k, other],
            device_id=at_x(x, mate),
            device_id_type=MESH,
        )

    def x_copy(k, d):
        other = turn(x, d, X)
        return pltpu.make_async_remote_copy(
            src_ref=partial.at[k, other * 2 + core],
            dst_ref=x_buf.at[k, d - 1],
            send_sem=x_send.at[k, d - 1],
            recv_sem=x_recv.at[k, d - 1],
            device_id=at_x(other, core),
            device_id_type=MESH,
        )

    def load_dense(p, slot, sem):
        return pltpu.make_async_copy(
            dense.at[pl.ds(p * nodes, nodes), :], panels.at[slot], dense_sem.at[sem]
        )

    def load_weights():
        return (
            pltpu.make_async_copy(w_in, w_in_v, w_sem.at[0]),
            pltpu.make_async_copy(w_out, w_out_v, w_sem.at[1]),
        )

    def pick(k, source, row_list):
        name = jnp.broadcast_to(row_list, (edge, width))
        value = zbuf[k, source, pl.ds(0, edge), :]
        for b in range(1, B):
            value = jnp.where(name == b, zbuf[k, source, pl.ds(b * edge, edge), :], value)
        return value

    def send_y(k, source):
        for d in range(1, Y):
            for j in range(J):
                entry = (source * Y + y) * J + j
                ysend_buf[k, d - 1, source, pl.ds(j * edge, edge), :] = pick(
                    k, source, asked[d - 1, pl.ds(entry, 1), :]
                )
            y_copy(k, d, source).start()

    def send_own(k):
        local_features(k).wait()

        @pl.when(z < Z - 1)
        def _():
            to_right(k, z).start()

        @pl.when(z > 0)
        def _():
            to_left(k, z).start()

    for k in range(chunks):
        local_features(k).start()
    barrier = pltpu.get_barrier_semaphore()

    @pl.when(z < Z - 1)
    def _():
        pl.semaphore_signal(barrier, inc=1, device_id=at_z(z + 1), device_id_type=MESH)

    @pl.when(z > 0)
    def _():
        pl.semaphore_signal(barrier, inc=1, device_id=at_z(z - 1), device_id_type=MESH)

    for d in range(1, Y):
        pl.semaphore_signal(barrier, inc=1, device_id=at_y(turn(y, d, Y)), device_id_type=MESH)
    for d in range(1, X):
        pl.semaphore_signal(
            barrier, inc=1, device_id=at_x(turn(x, d, X), core), device_id_type=MESH
        )
    pl.semaphore_signal(barrier, inc=1, device_id=at_x(x, mate), device_id_type=MESH)
    fixed = (Y - 1) + (X - 1) + 1
    pl.semaphore_wait(
        barrier, fixed + jnp.where(z < Z - 1, 1, 0) + jnp.where(z > 0, 1, 0)
    )

    for d in range(1, Y):
        ask_copy(d).start()
    for k in range(min(2, chunks)):
        send_own(k)
    if resident:
        for p in range(owners):
            load_dense(p, p, p).start()
    for copy in load_weights():
        copy.start()
    for d in range(1, Y):
        ask_copy(d).wait_recv()

    def gather(k):
        send_y(k, z)
        for h in range(1, Z):

            @pl.when(z >= h)
            def _():
                to_right(k, z - h).wait_recv()

                @pl.when(z < Z - 1)
                def _():
                    to_right(k, z - h).start()

            @pl.when(z + h < Z)
            def _():
                to_left(k, z + h).wait_recv()

                @pl.when(z > 0)
                def _():
                    to_left(k, z + h).start()

            @pl.when(z >= h)
            def _():
                send_y(k, z - h)

            @pl.when(z + h < Z)
            def _():
                send_y(k, z + h)

        @pl.when(k + 2 < chunks)
        def _():
            send_own(k + 2)

    def multiply(k):
        for source in range(Z):
            for j in range(J):
                entry = (source * Y + y) * J + j
                pool[pl.ds(pl.multiple_of(entry * edge, edge), edge), :] = pick(
                    k, source, wanted[pl.ds(entry, 1), :]
                ).astype(jnp.bfloat16)
        for d in range(1, Y):
            for source in range(Z):
                y_copy(k, d, source).wait_recv()
                entry = (source * Y + turn(y, d, Y)) * J
                pool[pl.ds(pl.multiple_of(entry * edge, J * edge), J * edge), :] = yrecv_buf[
                    k, d - 1, source
                ].astype(jnp.bfloat16)
        for which in (mate, core):

            def one(other, carry):
                p = other * 2 + which
                if resident:

                    @pl.when(k == 0)
                    def _():
                        load_dense(p, p, p).wait()

                    slot = p
                else:
                    load_dense(p, 0, 0).start()
                    load_dense(p, 0, 0).wait()
                    slot = 0
                partial[k, p] = jnp.dot(
                    panels[slot], pool[...], preferred_element_type=jnp.float32
                )
                if which is mate:
                    core_copy(k, other).start()
                return carry

            lax.fori_loop(0, X, one, 0)

    def reduce(k):
        for d in [*range(1, X), 0]:
            other = turn(x, d, X)
            core_copy(k, other).wait_recv()
            mine = other * 2 + core
            partial[k, mine] = partial[k, mine] + core_buf[k, other]
            if d:
                x_copy(k, d).start()

    def finish(k):
        total = partial[k, col]
        for d in range(1, X):
            x_copy(k, d).wait_recv()
            total = total + x_buf[k, d - 1]
        value = (1.0 + gin_epsilon) * zbuf[k, z] + total
        mixed[:, pl.ds(pl.multiple_of(k * width, width), width)] = value.astype(jnp.bfloat16)

    def stage(k, carry):
        @pl.when(k < chunks)
        def _():
            gather(k)

        @pl.when((k >= 2) & (k - 2 < chunks))
        def _():
            reduce(k - 2)

        @pl.when(k >= 3)
        def _():
            finish(k - 3)

        @pl.when((k >= 1) & (k - 1 < chunks))
        def _():
            multiply(k - 1)

        return carry

    lax.fori_loop(0, chunks + 3, stage, 0)

    for copy in load_weights():
        copy.wait()
    hidden_total = w_in_v.shape[1]
    step = math.gcd(512, hidden_total)
    result = jnp.broadcast_to(bias_out[...], (nodes, w_out_v.shape[1]))
    for h in range(hidden_total // step):
        part = pl.ds(h * step, step)
        hidden = jnp.dot(mixed[...], w_in_v[:, part], preferred_element_type=jnp.float32)
        hidden = jnp.maximum(hidden + bias_in[:, part], 0.0).astype(jnp.bfloat16)
        result = result + jnp.dot(hidden, w_out_v[part, :], preferred_element_type=jnp.float32)
    out[...] = result.astype(jnp.bfloat16)

    def drain(k, carry):
        for source in range(Z):

            @pl.when((z < Z - 1) & (z >= source))
            def _():
                to_right(k, source).wait_send()

            @pl.when((z > 0) & (z <= source))
            def _():
                to_left(k, source).wait_send()

            for d in range(1, Y):
                y_copy(k, d, source).wait_send()
        for other in range(X):
            core_copy(k, other).wait_send()
        for d in range(1, X):
            x_copy(k, d).wait_send()
        return carry

    lax.fori_loop(0, chunks, drain, 0)
    for d in range(1, Y):
        ask_copy(d).wait_send()


def layer(features, wanted, dense, w_in, bias_in, w_out, bias_out, edge):
    nodes, feat = features.shape
    grid_rows, J = wanted.shape
    cols = lax.axis_size("col")
    Y = max(d for d in range(1, math.isqrt(grid_rows) + 1) if grid_rows % d == 0)
    Z = grid_rows // Y
    X = cols // 2
    B = nodes // edge
    width = 128
    C = feat // width
    owners = 2 * X
    depth = dense.shape[1]
    hid = w_in.shape[1]
    resident = dense.size * 2 <= 16 * MIB
    slots = owners if resident else 1
    cfg = (Z, Y, X, J, B, edge, width, C, resident)
    names = jnp.broadcast_to(wanted.reshape(grid_rows * J, 1), (grid_rows * J, width))
    f32, bf16 = jnp.float32, jnp.bfloat16
    dma = pltpu.SemaphoreType.DMA
    y_peers, x_peers = max(Y - 1, 1), max(X - 1, 1)
    vmem = pl.BlockSpec(memory_space=pltpu.VMEM)
    hbm = pl.BlockSpec(memory_space=pl.ANY)
    return pl.pallas_call(
        functools.partial(layer_kernel, cfg),
        out_shape=jax.ShapeDtypeStruct((nodes, feat), bf16),
        in_specs=[hbm, vmem, hbm, hbm, vmem, hbm, vmem],
        out_specs=vmem,
        scratch_shapes=[
            pltpu.VMEM((C, Z, nodes, width), f32),
            pltpu.VMEM((C, y_peers, Z, J * edge, width), f32),
            pltpu.VMEM((C, y_peers, Z, J * edge, width), f32),
            pltpu.VMEM((y_peers, grid_rows * J, width), jnp.int32),
            pltpu.VMEM((slots, nodes, depth), bf16),
            pltpu.VMEM((depth, width), bf16),
            pltpu.VMEM((C, owners, nodes, width), f32),
            pltpu.VMEM((C, X, nodes, width), f32),
            pltpu.VMEM((C, x_peers, nodes, width), f32),
            pltpu.VMEM(w_in.shape, bf16),
            pltpu.VMEM(w_out.shape, bf16),
            pltpu.VMEM((nodes, feat), bf16),
            dma((C,)),
            dma((slots,)),
            dma((2,)),
            dma((C, Z)),
            dma((C, Z)),
            dma((C, Z)),
            dma((C, y_peers, Z)),
            dma((C, y_peers, Z)),
            dma((y_peers,)),
            dma((y_peers,)),
            dma((C, X)),
            dma((C, X)),
            dma((C, x_peers)),
            dma((C, x_peers)),
        ],
        compiler_params=pltpu.CompilerParams(
            collective_id=0, has_side_effects=True, vmem_limit_bytes=56 * MIB
        ),
        name="layer",
    )(features, names, dense, w_in, bias_in.reshape(1, hid), w_out, bias_out.reshape(1, feat))


def on_device(
    features, tiles, tile_rows, tile_cols, tile_count, needed, w_in, bias_in, w_out, bias_out
):
    edge = tiles.shape[-1]
    targets = lax.axis_size("col") * (features.shape[0] // edge)
    wanted = needed[0, 0]
    dense = assemble(
        tiles[0, 0], tile_rows[0, 0], tile_cols[0, 0], tile_count[0], targets, wanted.size
    )
    return layer(features, wanted, dense, w_in, bias_in, w_out, bias_out, edge)


def solution(mesh):
    placed = (
        P(("row", "col"), None),
        P("row", "col", None, None, None),
        P("row", "col", None),
        P("row", "col", None),
        P("row", "col"),
        P("row", "col", None, None),
        P(),
        P(),
        P(),
        P(),
    )
    return jax.shard_map(
        on_device, mesh=mesh, in_specs=placed, out_specs=P(("row", "col"), None), check_vma=False
    )
```

time: 325 us -> 115 us (0.35)
  waiting for transfers between devices: 135 us -> 0 us
  Pallas kernels: 0 us -> 106 us
  matrix products: 82.1 us -> 0 us
  local copies, waits for them, and re-layouts: 68.6 us -> 7.91 us
  blocking collectives: 13.5 us -> 0 us
  between operations: 14.1 us -> 0.68 us
  other arithmetic: 5.92 us -> 0 us
  starting transfers between devices: 4.76 us -> 0 us
    pallas_call x0 -> x2, Pallas kernels: none -> 106 us  [the longest x1 97.3 us: layer(): pl.pallas_call(functools.partial(layer_kernel, cfg), out_shape=jax.ShapeD...]
    all_to_all x1 -> x0, waiting for transfers between devices: 91.3 us -> none  [on_device(): lax.all_to_all(chosen, 'row', split_axis=0, concat_axis=0, tiled=True)]
    dot_general x9 -> x0, matrix products: 82.1 us -> none  [the longest x4 43.6 us: add_group(): jnp.einsum('tpq,tqf->tpf', group_tiles, inputs, precision=precise_mode)]
    reduce_scatter x1 -> x0, waiting for transfers between devices: 43.7 us -> none  [on_device(): lax.psum_scatter(partial_value.reshape(row_blocks * tile_edge, width), 'c...]
    while x4 -> x0, local copies, waits for them, and re-layouts: 32.4 us -> none
    gather x5 -> x0, local copies, waits for them, and re-layouts: 30.1 us -> none  [the longest x4 26 us: add_group(): inputs = jnp.take(column_pool, group_pos, axis=0)]
    all_to_all x1 -> x0, blocking collectives: 13.5 us -> none  [on_device(): lax.all_to_all(wanted, 'row', split_axis=0, concat_axis=0, tiled=True)]
    unnamed x12 -> x8, local copies, waits for them, and re-layouts: 0.02 us -> 7.15 us
  transfers between devices with their start and end apart: 2 -> 0, of which waited for: 2 -> 0; matrix products, arithmetic and copies ran while one was open for 0% -> 0% of each run, Pallas kernels for 0% -> 0%
where the time goes in v1:
time: 115 us; the launch traced here: 114 us
  Pallas kernels  106 us (92%)
  local copies, waits for them, and re-layouts  7.91 us (7%)
    pallas_call x1, Pallas kernels, layer(): pl.pallas_call(functools.partial(layer_kernel, cfg), out_shape=jax.ShapeD...  97.3 us
    pallas_call x1, Pallas kernels, assemble(): pl.pallas_call(assemble_kernel, out_shape=jax.ShapeDtypeStruct((targets *...  8.43 us
    unnamed x8, local copies, waits for them, and re-layouts  7.15 us

profile of v1, /device:TPU:0, one launch (start us, length us, event | category | flops | bytes accessed | tf_op | source)
XLA Modules:
  0.0 114.3 jit_solution(15328884049433711316)
XLA Ops:
  0.7 0.8 copy.12
  1.4 0.1 broadcast_in_dim.7
  1.5 0.7 broadcast_in_dim.8.wanted
  2.2 0.0 copy-start.1
  2.2 0.7 copy-done.1
  2.8 0.0 copy-start.2
  2.8 0.7 copy-done.2
  3.5 8.4 %assemble.1.dense = bf16[2048,2048]{1,0:T(8,128)(2,1)S(1)} custom-call(s32[128]{0:T(128)S(1)} %bitcast.9, s32[128]{0:T(128)S(1)} %bitcast.10, s32[1]{0:T(128)} %bitcast.8.count, f32[128,128,128]{2,1,0:T(8,128)} %bitcast.11), custom_call_target="tpu_custom_call" | custom-call | tf_op jit(solution)/shard_map/assemble/pallas_call | solution.py:41
  11.9 0.0 copy-start
  11.9 3.2 %copy-done = bf16[2048,2048]{1,0:T(8,128)(2,1)} copy-done((bf16[2048,2048]{1,0:T(8,128)(2,1)}, bf16[2048,2048]{1,0:T(8,128)(2,1)S(1)}, u32[]{:S(2)}) %copy-start) | copy-done | bytes 8388632
  15.1 97.3 %layer.1 = bf16[512,512]{1,0:T(8,128)(2,1)} custom-call(f32[512,512]{1,0:T(8,128)} %features.1, s32[16,128]{1,0:T(8,128)} %broadcast_in_dim.8.wanted, bf16[2048,2048]{1,0:T(8,128)(2,1)} %copy-done, bf16[512,2048]{1,0:T(8,128)(2,1)} %w_in.1, f32[1,2048]{1,0:T(1,128)} %bitcast.12, bf16[2048,512]{1,0:T(8,128)(2,1)} %w_out.1, f32[1,512]{1,0:T(1,128)} %bitcast.13), custom_call_target="tpu_custom_call" | custom-call | tf_op jit(solution)/shard_map/layer/pallas_call | solution.py:417
  112.4 1.9 %copy.15 = bf16[512,512]{1,0:T(8,128)(2,1)} copy(bf16[512,512]{1,0:T(8,128)(2,1)} %layer.1) | data formatting | bytes 1048576
Async XLA Ops:
  2.2 0.7 copy-start.1
  2.8 0.7 copy-start.2
  11.9 3.2 %copy-start = (bf16[2048,2048]{1,0:T(8,128)(2,1)}, bf16[2048,2048]{1,0:T(8,128)(2,1)S(1)}, u32[]{:S(2)}) copy-start(bf16[2048,2048]{1,0:T(8,128)(2,1)S(1)} %assemble.1.dense) | copy-start | bytes 25165828

commit v2 on v1

--- a/solution.py
+++ b/solution.py
@@ -49,6 +49,9 @@
             scratch_shapes=[pltpu.VMEM((height, slots * edge), jnp.float32)],
         ),
         compiler_params=pltpu.CompilerParams(vmem_limit_bytes=40 * MIB),
+        cost_estimate=pl.CostEstimate(
+            flops=0, bytes_accessed=8 * targets * slots * edge * edge, transcendentals=0
+        ),
         name="assemble",
     )(rows, cols, count, tiles)
 
@@ -56,6 +59,8 @@
 def layer_kernel(
     cfg,
     features,
+    from_left,
+    from_right,
     wanted,
     dense,
     w_in,
@@ -110,11 +115,13 @@
     def at_x(other, which):
         return (row, other * 2 + which)
 
-    def local_features(k):
+    def local_copy(k, which):
         return pltpu.make_async_copy(
-            features.at[:, pl.ds(pl.multiple_of(k * width, width), width)],
-            zbuf.at[k, z],
-            feat_sem.at[k],
+            (features, from_left, from_right)[which].at[
+                :, pl.ds(pl.multiple_of(k * width, width), width)
+            ],
+            zbuf.at[k, (z, z - 1, z + 1)[which]],
+            feat_sem.at[which, k],
         )
 
     def z_copy(k, source, to, sem):
@@ -201,19 +208,19 @@
                 )
             y_copy(k, d, source).start()
 
-    def send_own(k):
-        local_features(k).wait()
-
-        @pl.when(z < Z - 1)
-        def _():
-            to_right(k, z).start()
-
-        @pl.when(z > 0)
-        def _():
-            to_left(k, z).start()
-
+    has_left, has_right = z > 0, z < Z - 1
     for k in range(chunks):
-        local_features(k).start()
+
+        @pl.when(has_left)
+        def _():
+            local_copy(k, 1).start()
+
+        @pl.when(has_right)
+        def _():
+            local_copy(k, 2).start()
+
+    for k in range(chunks):
+        local_copy(k, 0).start()
     barrier = pltpu.get_barrier_semaphore()
 
     @pl.when(z < Z - 1)
@@ -238,8 +245,27 @@
 
     for d in range(1, Y):
         ask_copy(d).start()
-    for k in range(min(2, chunks)):
-        send_own(k)
+
+    def first_forward(k, carry):
+        @pl.when(has_left)
+        def _():
+            local_copy(k, 1).wait()
+
+            @pl.when(has_right)
+            def _():
+                to_right(k, z - 1).start()
+
+        @pl.when(has_right)
+        def _():
+            local_copy(k, 2).wait()
+
+            @pl.when(has_left)
+            def _():
+                to_left(k, z + 1).start()
+
+        return carry
+
+    lax.fori_loop(0, chunks, first_forward, 0)
     if resident:
         for p in range(owners):
             load_dense(p, p, p).start()
@@ -248,37 +274,57 @@
     for d in range(1, Y):
         ask_copy(d).wait_recv()
 
+    def near(k, carry):
+        local_copy(k, 0).wait()
+        send_y(k, z)
+
+        @pl.when(has_left)
+        def _():
+            send_y(k, z - 1)
+
+        @pl.when(has_right)
+        def _():
+            send_y(k, z + 1)
+
+        return carry
+
+    lax.fori_loop(0, chunks, near, 0)
+
+    def pass_on(k, h):
+        @pl.when(z >= h)
+        def _():
+            to_right(k, z - h).wait_recv()
+
+            @pl.when(has_right)
+            def _():
+                to_right(k, z - h).start()
+
+        @pl.when(z + h < Z)
+        def _():
+            to_left(k, z + h).wait_recv()
+
+            @pl.when(has_left)
+            def _():
+                to_left(k, z + h).start()
+
+        @pl.when(z >= h)
+        def _():
+            send_y(k, z - h)
+
+        @pl.when(z + h < Z)
+        def _():
+            send_y(k, z + h)
+
+    def far(k, carry):
+        for h in range(2, Z - 1):
+            pass_on(k, h)
+        return carry
+
+    lax.fori_loop(0, chunks, far, 0)
+
     def gather(k):
-        send_y(k, z)
-        for h in range(1, Z):
-
-            @pl.when(z >= h)
-            def _():
-                to_right(k, z - h).wait_recv()
-
-                @pl.when(z < Z - 1)
-                def _():
-                    to_right(k, z - h).start()
-
-            @pl.when(z + h < Z)
-            def _():
-                to_left(k, z + h).wait_recv()
-
-                @pl.when(z > 0)
-                def _():
-                    to_left(k, z + h).start()
-
-            @pl.when(z >= h)
-            def _():
-                send_y(k, z - h)
-
-            @pl.when(z + h < Z)
-            def _():
-                send_y(k, z + h)
-
-        @pl.when(k + 2 < chunks)
-        def _():
-            send_own(k + 2)
+        if Z > 2:
+            pass_on(k, Z - 1)
 
     def multiply(k):
         for source in range(Z):
@@ -294,9 +340,9 @@
                 pool[pl.ds(pl.multiple_of(entry * edge, J * edge), J * edge), :] = yrecv_buf[
                     k, d - 1, source
                 ].astype(jnp.bfloat16)
-        for which in (mate, core):
-
-            def one(other, carry):
+        def one(d, carry):
+            other = turn(x, d + 1, X)
+            for which in (mate, core):
                 p = other * 2 + which
                 if resident:
 
@@ -314,9 +360,9 @@
                 )
                 if which is mate:
                     core_copy(k, other).start()
-                return carry
-
-            lax.fori_loop(0, X, one, 0)
+            return carry
+
+        lax.fori_loop(0, X, one, 0)
 
     def reduce(k):
         for d in [*range(1, X), 0]:
@@ -371,11 +417,11 @@
     def drain(k, carry):
         for source in range(Z):
 
-            @pl.when((z < Z - 1) & (z >= source))
+            @pl.when((z < Z - 1) & (z > source))
             def _():
                 to_right(k, source).wait_send()
 
-            @pl.when((z > 0) & (z <= source))
+            @pl.when((z > 0) & (z < source))
             def _():
                 to_left(k, source).wait_send()
 
@@ -392,12 +438,16 @@
         ask_copy(d).wait_send()
 
 
-def layer(features, wanted, dense, w_in, bias_in, w_out, bias_out, edge):
+def row_grid(grid_rows):
+    inner = max(d for d in range(1, math.isqrt(grid_rows) + 1) if grid_rows % d == 0)
+    return grid_rows // inner, inner
+
+
+def layer(features, from_left, from_right, wanted, dense, w_in, bias_in, w_out, bias_out, edge):
     nodes, feat = features.shape
     grid_rows, J = wanted.shape
     cols = lax.axis_size("col")
-    Y = max(d for d in range(1, math.isqrt(grid_rows) + 1) if grid_rows % d == 0)
-    Z = grid_rows // Y
+    Z, Y = row_grid(grid_rows)
     X = cols // 2
     B = nodes // edge
     width = 128
@@ -417,7 +467,7 @@
     return pl.pallas_call(
         functools.partial(layer_kernel, cfg),
         out_shape=jax.ShapeDtypeStruct((nodes, feat), bf16),
-        in_specs=[hbm, vmem, hbm, hbm, vmem, hbm, vmem],
+        in_specs=[hbm, vmem, vmem, vmem, hbm, hbm, vmem, hbm, vmem],
         out_specs=vmem,
         scratch_shapes=[
             pltpu.VMEM((C, Z, nodes, width), f32),
@@ -432,7 +482,7 @@
             pltpu.VMEM(w_in.shape, bf16),
             pltpu.VMEM(w_out.shape, bf16),
             pltpu.VMEM((nodes, feat), bf16),
-            dma((C,)),
+            dma((3, C)),
             dma((slots,)),
             dma((2,)),
             dma((C, Z)),
@@ -448,10 +498,10 @@
             dma((C, x_peers)),
         ],
         compiler_params=pltpu.CompilerParams(
-            collective_id=0, has_side_effects=True, vmem_limit_bytes=56 * MIB
+            collective_id=0, has_side_effects=True, vmem_limit_bytes=(40 if resident else 56) * MIB
         ),
         name="layer",
-    )(features, names, dense, w_in, bias_in.reshape(1, hid), w_out, bias_out.reshape(1, feat))
+    )(features, from_left, from_right, names, dense, w_in, bias_in.reshape(1, hid), w_out, bias_out.reshape(1, feat))
 
 
 def on_device(
@@ -460,10 +510,14 @@
     edge = tiles.shape[-1]
     targets = lax.axis_size("col") * (features.shape[0] // edge)
     wanted = needed[0, 0]
+    Z, Y = row_grid(lax.axis_size("row"))
+    pairs = [(r, r + Y) for r in range((Z - 1) * Y)]
+    from_left = lax.ppermute(features, "row", pairs)
+    from_right = lax.ppermute(features, "row", [(b, a) for a, b in pairs])
     dense = assemble(
         tiles[0, 0], tile_rows[0, 0], tile_cols[0, 0], tile_count[0], targets, wanted.size
     )
-    return layer(features, wanted, dense, w_in, bias_in, w_out, bias_out, edge)
+    return layer(features, from_left, from_right, wanted, dense, w_in, bias_in, w_out, bias_out, edge)
 
 
 def solution(mesh):

time: 115 us -> 109 us (0.948)
  Pallas kernels: 106 us -> 87.7 us
  waiting for transfers between devices: 0 us -> 7.98 us
  starting transfers between devices: 0 us -> 6.28 us
  local copies, waits for them, and re-layouts: 7.91 us -> 6.25 us
    pallas_call x1, Pallas kernels: 97.3 us -> 76.3 us  [layer(): pl.pallas_call(functools.partial(layer_kernel, cfg), out_shape=jax.ShapeD...]
    ppermute x0 -> x2, waiting for transfers between devices: none -> 7.98 us  [the longest x1 4.08 us: on_device(): from_right = lax.ppermute(features, 'row', [(b, a) for a, b in pairs])]
    ppermute x0 -> x2, starting transfers between devices: none -> 6.28 us  [the longest x1 4.98 us: on_device(): from_left = lax.ppermute(features, 'row', pairs)]
    pallas_call x1, Pallas kernels: 8.43 us -> 11.4 us  [assemble(): pl.pallas_call(assemble_kernel, out_shape=jax.ShapeDtypeStruct((targets *...]
    unnamed x8 -> x18, local copies, waits for them, and re-layouts: 7.15 us -> 6.1 us
  transfers between devices with their start and end apart: 0 -> 2, of which waited for: 0 -> 2; matrix products, arithmetic and copies ran while one was open for 0% -> 1% of each run, Pallas kernels for 0% -> 10%
where the time goes in v2:
time: 109 us
  Pallas kernels  87.7 us (80%)
  waiting for transfers between devices  7.98 us (7%)
  starting transfers between devices  6.28 us (6%)
  local copies, waits for them, and re-layouts  6.25 us (6%)
    pallas_call x1, Pallas kernels, layer(): pl.pallas_call(functools.partial(layer_kernel, cfg), out_shape=jax.ShapeD...  76.3 us
    pallas_call x1, Pallas kernels, assemble(): pl.pallas_call(assemble_kernel, out_shape=jax.ShapeDtypeStruct((targets *...  11.4 us
    unnamed x18, local copies, waits for them, and re-layouts  6.1 us
    ppermute x1, starting transfers between devices, on_device(): from_left = lax.ppermute(features, 'row', pairs)  4.98 us
    ppermute x1, waiting for transfers between devices, on_device(): from_right = lax.ppermute(features, 'row', [(b, a) for a, b in pairs])  4.08 us
    ppermute x1, waiting for transfers between devices, on_device(): from_left = lax.ppermute(features, 'row', pairs)  3.9 us
  transfers between devices with their start and end apart: 2, of which 2 were waited for; matrix products, arithmetic and copies ran while one was open for 1% of the time, Pallas kernels for 10%

profile of v2, /device:TPU:0, one launch (start us, length us, event | category | flops | bytes accessed | tf_op | source)
XLA Modules:
  0.0 108.9 jit_solution(12838067827553190659)
XLA Ops:
  0.0 5.0 %collective-permute-start = (f32[512,512]{1,0:T(8,128)}, f32[512,512]{1,0:T(8,128)S(1)}, u32[]{:S(2)}, u32[]{:S(2)}) collective-permute-start(f32[512,512]{1,0:T(8,128)} %features.1), channel_id=1, source_target_pairs={{0,8},{4,12},{8,16},{12,20},{16,24},{20,28},{1,9},{5,13},{9,17},{1... | collective-permute-start | bytes 3145736 | tf_op jit(solution)/shard_map/ppermute | solution.py:515
  5.0 1.3 %collective-permute-start.1 = (f32[512,512]{1,0:T(8,128)}, f32[512,512]{1,0:T(8,128)S(1)}, u32[]{:S(2)}, u32[]{:S(2)}) collective-permute-start(f32[512,512]{1,0:T(8,128)} %features.1), channel_id=1, source_target_pairs={{8,0},{12,4},{16,8},{20,12},{24,16},{28,20},{9,1},{13,5},{17,9},{2... | collective-permute-start | bytes 3145736 | tf_op jit(solution)/shard_map/ppermute | solution.py:516
  6.9 0.8 copy.12
  7.7 0.1 broadcast_in_dim.7
  7.8 0.0 copy-start.6
  7.8 0.7 copy-done.6
  8.4 0.0 copy-start.7
  8.4 0.7 copy-done.7
  9.1 0.0 copy-start.1
  9.1 0.0 copy-start.2
  9.1 0.0 copy-start.5
  9.1 11.4 %assemble.1.dense = bf16[2048,2048]{1,0:T(8,128)(2,1)S(1)} custom-call(s32[128]{0:T(128)S(1)} %bitcast.11, s32[128]{0:T(128)S(1)} %bitcast.12, s32[1]{0:T(128)} %bitcast.8.count, f32[128,128,128]{2,1,0:T(8,128)} %bitcast.13), custom_call_target="tpu_custom_call" | custom-call | bytes 33554432 | tf_op jit(solution)/shard_map/assemble/pallas_call | solution.py:41
  20.5 0.0 copy-start
  20.5 3.2 %copy-done = bf16[2048,2048]{1,0:T(8,128)(2,1)} copy-done((bf16[2048,2048]{1,0:T(8,128)(2,1)}, bf16[2048,2048]{1,0:T(8,128)(2,1)S(1)}, u32[]{:S(2)}) %copy-start) | copy-done | bytes 8388632
  23.7 3.9 %collective-permute-done.from_left = f32[512,512]{1,0:T(8,128)S(1)} collective-permute-done((f32[512,512]{1,0:T(8,128)}, f32[512,512]{1,0:T(8,128)S(1)}, u32[]{:S(2)}, u32[]{:S(2)}) %collective-permute-start) | collective-permute-done | bytes 1048608 | tf_op jit(solution)/shard_map/ppermute | solution.py:515
  27.6 4.1 %collective-permute-done.1.from_right = f32[512,512]{1,0:T(8,128)S(1)} collective-permute-done((f32[512,512]{1,0:T(8,128)}, f32[512,512]{1,0:T(8,128)S(1)}, u32[]{:S(2)}, u32[]{:S(2)}) %collective-permute-start.1) | collective-permute-done | bytes 1048608 | tf_op jit(solution)/shard_map/ppermute | solution.py:516
  31.7 0.1 broadcast_in_dim.8.wanted
  31.8 0.0 copy-done.1
  31.8 0.0 copy-done.2
  31.8 0.0 copy-done.3
  31.8 0.0 copy-done.4
  31.8 0.0 copy-done.5
  31.8 76.3 %layer.1 = bf16[512,512]{1,0:T(8,128)(2,1)S(1)} custom-call(f32[512,512]{1,0:T(8,128)S(1)} %copy-done.3, f32[512,512]{1,0:T(8,128)S(1)} %collective-permute-done.from_left, f32[512,512]{1,0:T(8,128)S(1)} %collective-permute-done.1.from_right, s32[16,128]{1,0:T(8,128)S(1)} %broadcast_in_dim.8.wanted, bf16[2048,2048]{1,0:T(8,128)(2,1)} %copy-done, ...), custom_call_target="tpu_custom_call" | custom-call | tf_op jit(solution)/shard_map/layer/pallas_call | solution.py:467
  108.1 0.8 copy.15
  (2 shorter events, 0.0 us)
Async XLA Ops:
  0.0 27.6 %collective-permute-start = (f32[512,512]{1,0:T(8,128)}, f32[512,512]{1,0:T(8,128)S(1)}, u32[]{:S(2)}, u32[]{:S(2)}) collective-permute-start(f32[512,512]{1,0:T(8,128)} %features.1), channel_id=1, source_target_pairs={{0,8},{4,12},{8,16},{12,20},{16,24},{20,28},{1,9},{5,13},{9,17},{1... | collective-permute-start | bytes 3145736 | tf_op jit(solution)/shard_map/ppermute | solution.py:515
  5.0 26.7 %collective-permute-start.1 = (f32[512,512]{1,0:T(8,128)}, f32[512,512]{1,0:T(8,128)S(1)}, u32[]{:S(2)}, u32[]{:S(2)}) collective-permute-start(f32[512,512]{1,0:T(8,128)} %features.1), channel_id=1, source_target_pairs={{8,0},{12,4},{16,8},{20,12},{24,16},{28,20},{9,1},{13,5},{17,9},{2... | collective-permute-start | bytes 3145736 | tf_op jit(solution)/shard_map/ppermute | solution.py:516
  7.8 0.7 copy-start.6
  8.4 0.7 copy-start.7
  9.1 22.7 %copy-start.1 = (bf16[512,2048]{1,0:T(8,128)(2,1)S(1)}, bf16[512,2048]{1,0:T(8,128)(2,1)}, u32[]{:S(2)}) copy-start(bf16[512,2048]{1,0:T(8,128)(2,1)} %w_in.1) | copy-start | bytes 6291460
  9.1 22.7 %copy-start.2 = (bf16[2048,512]{1,0:T(8,128)(2,1)S(1)}, bf16[2048,512]{1,0:T(8,128)(2,1)}, u32[]{:S(2)}) copy-start(bf16[2048,512]{1,0:T(8,128)(2,1)} %w_out.1) | copy-start | bytes 6291460
  9.1 22.7 %copy-start.3 = (f32[512,512]{1,0:T(8,128)S(1)}, f32[512,512]{1,0:T(8,128)}, u32[]{:S(2)}) copy-start(f32[512,512]{1,0:T(8,128)} %features.1) | copy-start | bytes 3145732
  9.1 22.7 %copy-start.4 = (f32[2048]{0:T(1024)S(1)}, f32[2048]{0:T(1024)}, u32[]{:S(2)}) copy-start(f32[2048]{0:T(1024)} %param.17) | copy-start | bytes 24580
  9.1 22.7 %copy-start.5 = (f32[512]{0:T(512)S(1)}, f32[512]{0:T(512)}, u32[]{:S(2)}) copy-start(f32[512]{0:T(512)} %param.19) | copy-start | bytes 6148
  20.5 3.2 %copy-start = (bf16[2048,2048]{1,0:T(8,128)(2,1)}, bf16[2048,2048]{1,0:T(8,128)(2,1)S(1)}, u32[]{:S(2)}) copy-start(bf16[2048,2048]{1,0:T(8,128)(2,1)S(1)} %assemble.1.dense) | copy-start | bytes 25165828

commit v3 on v2

--- a/solution.py
+++ b/solution.py
@@ -246,7 +246,7 @@
     for d in range(1, Y):
         ask_copy(d).start()
 
-    def first_forward(k, carry):
+    def first_forward(k):
         @pl.when(has_left)
         def _():
             local_copy(k, 1).wait()
@@ -263,9 +263,8 @@
             def _():
                 to_left(k, z + 1).start()
 
-        return carry
-
-    lax.fori_loop(0, chunks, first_forward, 0)
+    for k in range(min(2, chunks)):
+        first_forward(k)
     if resident:
         for p in range(owners):
             load_dense(p, p, p).start()
@@ -274,7 +273,7 @@
     for d in range(1, Y):
         ask_copy(d).wait_recv()
 
-    def near(k, carry):
+    def near(k):
         local_copy(k, 0).wait()
         send_y(k, z)
 
@@ -285,10 +284,6 @@
         @pl.when(has_right)
         def _():
             send_y(k, z + 1)
-
-        return carry
-
-    lax.fori_loop(0, chunks, near, 0)
 
     def pass_on(k, h):
         @pl.when(z >= h)
@@ -315,16 +310,13 @@
         def _():
             send_y(k, z + h)
 
-    def far(k, carry):
-        for h in range(2, Z - 1):
+    def far(k):
+        for h in range(2, Z):
             pass_on(k, h)
-        return carry
-
-    lax.fori_loop(0, chunks, far, 0)
-
-    def gather(k):
-        if Z > 2:
-            pass_on(k, Z - 1)
+
+        @pl.when(k + 2 < chunks)
+        def _():
+            first_forward(k + 2)
 
     def multiply(k):
         for source in range(Z):
@@ -384,23 +376,24 @@
     def stage(k, carry):
         @pl.when(k < chunks)
         def _():
-            gather(k)
-
-        @pl.when((k >= 2) & (k - 2 < chunks))
-        def _():
-            reduce(k - 2)
-
-        @pl.when(k >= 3)
-        def _():
-            finish(k - 3)
+            near(k)
 
         @pl.when((k >= 1) & (k - 1 < chunks))
         def _():
             multiply(k - 1)
+            reduce(k - 1)
+
+        @pl.when(k < chunks)
+        def _():
+            far(k)
+
+        @pl.when(k >= 2)
+        def _():
+            finish(k - 2)
 
         return carry
 
-    lax.fori_loop(0, chunks + 3, stage, 0)
+    lax.fori_loop(0, chunks + 2, stage, 0)
 
     for copy in load_weights():
         copy.wait()

time: 109 us -> 114 us (1.046)
  waiting for transfers between devices: 7.98 us -> 12.5 us
    pallas_call x1, Pallas kernels: 76.3 us -> 81.3 us  [layer(): pl.pallas_call(functools.partial(layer_kernel, cfg), out_shape=jax.ShapeD...]
    pallas_call x1, Pallas kernels: 11.4 us -> 6.87 us  [assemble(): pl.pallas_call(assemble_kernel, out_shape=jax.ShapeDtypeStruct((targets *...]
    ppermute x1, waiting for transfers between devices: 3.9 us -> 8.42 us  [on_device(): from_left = lax.ppermute(features, 'row', pairs)]
  transfers between devices with their start and end apart: 2 -> 2, of which waited for: 2 -> 2; matrix products, arithmetic and copies ran while one was open for 1% -> 1% of each run, Pallas kernels for 10% -> 6%
where the time goes in v3:
time: 114 us
  Pallas kernels  88.2 us (77%)
  waiting for transfers between devices  12.5 us (11%)
  starting transfers between devices  6.28 us (6%)
  local copies, waits for them, and re-layouts  6.25 us (5%)
    pallas_call x1, Pallas kernels, layer(): pl.pallas_call(functools.partial(layer_kernel, cfg), out_shape=jax.ShapeD...  81.3 us
    ppermute x1, waiting for transfers between devices, on_device(): from_left = lax.ppermute(features, 'row', pairs)  8.42 us
    pallas_call x1, Pallas kernels, assemble(): pl.pallas_call(assemble_kernel, out_shape=jax.ShapeDtypeStruct((targets *...  6.87 us
    unnamed x18, local copies, waits for them, and re-layouts  6.1 us
    ppermute x1, starting transfers between devices, on_device(): from_left = lax.ppermute(features, 'row', pairs)  4.98 us
    ppermute x1, waiting for transfers between devices, on_device(): from_right = lax.ppermute(features, 'row', [(b, a) for a, b in pairs])  4.08 us
  transfers between devices with their start and end apart: 2, of which 2 were waited for; matrix products, arithmetic and copies ran while one was open for 1% of the time, Pallas kernels for 6%

profile of v3, /device:TPU:0, one launch (start us, length us, event | category | flops | bytes accessed | tf_op | source)
XLA Modules:
  0.0 113.9 jit_solution(7009043663771294944)
XLA Ops:
  0.0 5.0 %collective-permute-start = (f32[512,512]{1,0:T(8,128)}, f32[512,512]{1,0:T(8,128)S(1)}, u32[]{:S(2)}, u32[]{:S(2)}) collective-permute-start(f32[512,512]{1,0:T(8,128)} %features.1), channel_id=1, source_target_pairs={{0,8},{4,12},{8,16},{12,20},{16,24},{20,28},{1,9},{5,13},{9,17},{1... | collective-permute-start | bytes 3145736 | tf_op jit(solution)/shard_map/ppermute | solution.py:508
  5.0 1.3 %collective-permute-start.1 = (f32[512,512]{1,0:T(8,128)}, f32[512,512]{1,0:T(8,128)S(1)}, u32[]{:S(2)}, u32[]{:S(2)}) collective-permute-start(f32[512,512]{1,0:T(8,128)} %features.1), channel_id=1, source_target_pairs={{8,0},{12,4},{16,8},{20,12},{24,16},{28,20},{9,1},{13,5},{17,9},{2... | collective-permute-start | bytes 3145736 | tf_op jit(solution)/shard_map/ppermute | solution.py:509
  6.9 0.8 copy.12
  7.7 0.1 broadcast_in_dim.7
  7.8 0.0 copy-start.6
  7.8 0.7 copy-done.6
  8.4 0.0 copy-start.7
  8.4 0.7 copy-done.7
  9.1 0.0 copy-start.2
  9.1 0.0 copy-start.3
  9.1 0.0 copy-start.5
  9.1 6.9 %assemble.1.dense = bf16[2048,2048]{1,0:T(8,128)(2,1)S(1)} custom-call(s32[128]{0:T(128)S(1)} %bitcast.11, s32[128]{0:T(128)S(1)} %bitcast.12, s32[1]{0:T(128)} %bitcast.8.count, f32[128,128,128]{2,1,0:T(8,128)} %bitcast.13), custom_call_target="tpu_custom_call" | custom-call | bytes 33554432 | tf_op jit(solution)/shard_map/assemble/pallas_call | solution.py:41
  16.0 0.0 copy-start
  16.0 3.2 %copy-done = bf16[2048,2048]{1,0:T(8,128)(2,1)} copy-done((bf16[2048,2048]{1,0:T(8,128)(2,1)}, bf16[2048,2048]{1,0:T(8,128)(2,1)S(1)}, u32[]{:S(2)}) %copy-start) | copy-done | bytes 8388632
  19.2 8.4 %collective-permute-done.from_left = f32[512,512]{1,0:T(8,128)S(1)} collective-permute-done((f32[512,512]{1,0:T(8,128)}, f32[512,512]{1,0:T(8,128)S(1)}, u32[]{:S(2)}, u32[]{:S(2)}) %collective-permute-start) | collective-permute-done | bytes 1048608 | tf_op jit(solution)/shard_map/ppermute | solution.py:508
  27.6 4.1 %collective-permute-done.1.from_right = f32[512,512]{1,0:T(8,128)S(1)} collective-permute-done((f32[512,512]{1,0:T(8,128)}, f32[512,512]{1,0:T(8,128)S(1)}, u32[]{:S(2)}, u32[]{:S(2)}) %collective-permute-start.1) | collective-permute-done | bytes 1048608 | tf_op jit(solution)/shard_map/ppermute | solution.py:509
  31.7 0.1 broadcast_in_dim.8.wanted
  31.8 0.0 copy-done.1
  31.8 0.0 copy-done.2
  31.8 0.0 copy-done.3
  31.8 0.0 copy-done.4
  31.8 0.0 copy-done.5
  31.8 81.3 %layer.1 = bf16[512,512]{1,0:T(8,128)(2,1)S(1)} custom-call(f32[512,512]{1,0:T(8,128)S(1)} %copy-done.3, f32[512,512]{1,0:T(8,128)S(1)} %collective-permute-done.from_left, f32[512,512]{1,0:T(8,128)S(1)} %collective-permute-done.1.from_right, s32[16,128]{1,0:T(8,128)S(1)} %broadcast_in_dim.8.wanted, bf16[2048,2048]{1,0:T(8,128)(2,1)} %copy-done, ...), custom_call_target="tpu_custom_call" | custom-call | tf_op jit(solution)/shard_map/layer/pallas_call | solution.py:460
  113.1 0.8 copy.15
  (2 shorter events, 0.0 us)
Async XLA Ops:
  0.0 27.6 %collective-permute-start = (f32[512,512]{1,0:T(8,128)}, f32[512,512]{1,0:T(8,128)S(1)}, u32[]{:S(2)}, u32[]{:S(2)}) collective-permute-start(f32[512,512]{1,0:T(8,128)} %features.1), channel_id=1, source_target_pairs={{0,8},{4,12},{8,16},{12,20},{16,24},{20,28},{1,9},{5,13},{9,17},{1... | collective-permute-start | bytes 3145736 | tf_op jit(solution)/shard_map/ppermute | solution.py:508
  5.0 26.7 %collective-permute-start.1 = (f32[512,512]{1,0:T(8,128)}, f32[512,512]{1,0:T(8,128)S(1)}, u32[]{:S(2)}, u32[]{:S(2)}) collective-permute-start(f32[512,512]{1,0:T(8,128)} %features.1), channel_id=1, source_target_pairs={{8,0},{12,4},{16,8},{20,12},{24,16},{28,20},{9,1},{13,5},{17,9},{2... | collective-permute-start | bytes 3145736 | tf_op jit(solution)/shard_map/ppermute | solution.py:509
  7.8 0.7 copy-start.6
  8.4 0.7 copy-start.7
  9.1 22.7 %copy-start.1 = (bf16[512,2048]{1,0:T(8,128)(2,1)S(1)}, bf16[512,2048]{1,0:T(8,128)(2,1)}, u32[]{:S(2)}) copy-start(bf16[512,2048]{1,0:T(8,128)(2,1)} %w_in.1) | copy-start | bytes 6291460
  9.1 22.7 %copy-start.2 = (bf16[2048,512]{1,0:T(8,128)(2,1)S(1)}, bf16[2048,512]{1,0:T(8,128)(2,1)}, u32[]{:S(2)}) copy-start(bf16[2048,512]{1,0:T(8,128)(2,1)} %w_out.1) | copy-start | bytes 6291460
  9.1 22.7 %copy-start.3 = (f32[512,512]{1,0:T(8,128)S(1)}, f32[512,512]{1,0:T(8,128)}, u32[]{:S(2)}) copy-start(f32[512,512]{1,0:T(8,128)} %features.1) | copy-start | bytes 3145732
  9.1 22.7 %copy-start.4 = (f32[2048]{0:T(1024)S(1)}, f32[2048]{0:T(1024)}, u32[]{:S(2)}) copy-start(f32[2048]{0:T(1024)} %param.17) | copy-start | bytes 24580
  9.1 22.7 %copy-start.5 = (f32[512]{0:T(512)S(1)}, f32[512]{0:T(512)}, u32[]{:S(2)}) copy-start(f32[512]{0:T(512)} %param.19) | copy-start | bytes 6148
  16.0 3.2 %copy-start = (bf16[2048,2048]{1,0:T(8,128)(2,1)}, bf16[2048,2048]{1,0:T(8,128)(2,1)S(1)}, u32[]{:S(2)}) copy-start(bf16[2048,2048]{1,0:T(8,128)(2,1)S(1)} %assemble.1.dense) | copy-start | bytes 25165828

commit v4 on v2

--- a/solution.py
+++ b/solution.py
@@ -274,7 +274,7 @@
     for d in range(1, Y):
         ask_copy(d).wait_recv()
 
-    def near(k, carry):
+    def near(k):
         local_copy(k, 0).wait()
         send_y(k, z)
 
@@ -285,10 +285,6 @@
         @pl.when(has_right)
         def _():
             send_y(k, z + 1)
-
-        return carry
-
-    lax.fori_loop(0, chunks, near, 0)
 
     def pass_on(k, h):
         @pl.when(z >= h)
@@ -316,6 +312,7 @@
             send_y(k, z + h)
 
     def far(k, carry):
+        near(k)
         for h in range(2, Z - 1):
             pass_on(k, h)
         return carry
@@ -386,21 +383,18 @@
         def _():
             gather(k)
 
-        @pl.when((k >= 2) & (k - 2 < chunks))
-        def _():
-            reduce(k - 2)
-
-        @pl.when(k >= 3)
-        def _():
-            finish(k - 3)
-
         @pl.when((k >= 1) & (k - 1 < chunks))
         def _():
             multiply(k - 1)
+            reduce(k - 1)
+
+        @pl.when(k >= 2)
+        def _():
+            finish(k - 2)
 
         return carry
 
-    lax.fori_loop(0, chunks + 3, stage, 0)
+    lax.fori_loop(0, chunks + 2, stage, 0)
 
     for copy in load_weights():
         copy.wait()

time: 109 us -> 109 us (level)
  waiting for transfers between devices: 7.98 us -> 11.6 us
  Pallas kernels: 87.7 us -> 84.1 us
    pallas_call x1, Pallas kernels: 11.4 us -> 7.82 us  [assemble(): pl.pallas_call(assemble_kernel, out_shape=jax.ShapeDtypeStruct((targets *...]
    ppermute x1, waiting for transfers between devices: 3.9 us -> 7.48 us  [on_device(): from_left = lax.ppermute(features, 'row', pairs)]
  transfers between devices with their start and end apart: 2 -> 2, of which waited for: 2 -> 2; matrix products, arithmetic and copies ran while one was open for 1% -> 1% of each run, Pallas kernels for 10% -> 7%
where the time goes in v4:
time: 109 us
  Pallas kernels  84.1 us (77%)
  waiting for transfers between devices  11.6 us (11%)
  starting transfers between devices  6.28 us (6%)
  local copies, waits for them, and re-layouts  6.25 us (6%)
    pallas_call x1, Pallas kernels, layer(): pl.pallas_call(functools.partial(layer_kernel, cfg), out_shape=jax.ShapeD...  76.3 us
    pallas_call x1, Pallas kernels, assemble(): pl.pallas_call(assemble_kernel, out_shape=jax.ShapeDtypeStruct((targets *...  7.82 us
    ppermute x1, waiting for transfers between devices, on_device(): from_left = lax.ppermute(features, 'row', pairs)  7.48 us
    unnamed x18, local copies, waits for them, and re-layouts  6.1 us
    ppermute x1, starting transfers between devices, on_device(): from_left = lax.ppermute(features, 'row', pairs)  4.98 us
    ppermute x1, waiting for transfers between devices, on_device(): from_right = lax.ppermute(features, 'row', [(b, a) for a, b in pairs])  4.08 us
  transfers between devices with their start and end apart: 2, of which 2 were waited for; matrix products, arithmetic and copies ran while one was open for 1% of the time, Pallas kernels for 7%

profile of v4, /device:TPU:0, one launch (start us, length us, event | category | flops | bytes accessed | tf_op | source)
XLA Modules:
  0.0 109.0 jit_solution(12064091945079687633)
XLA Ops:
  0.0 5.0 %collective-permute-start = (f32[512,512]{1,0:T(8,128)}, f32[512,512]{1,0:T(8,128)S(1)}, u32[]{:S(2)}, u32[]{:S(2)}) collective-permute-start(f32[512,512]{1,0:T(8,128)} %features.1), channel_id=1, source_target_pairs={{0,8},{4,12},{8,16},{12,20},{16,24},{20,28},{1,9},{5,13},{9,17},{1... | collective-permute-start | bytes 3145736 | tf_op jit(solution)/shard_map/ppermute | solution.py:509
  5.0 1.3 %collective-permute-start.1 = (f32[512,512]{1,0:T(8,128)}, f32[512,512]{1,0:T(8,128)S(1)}, u32[]{:S(2)}, u32[]{:S(2)}) collective-permute-start(f32[512,512]{1,0:T(8,128)} %features.1), channel_id=1, source_target_pairs={{8,0},{12,4},{16,8},{20,12},{24,16},{28,20},{9,1},{13,5},{17,9},{2... | collective-permute-start | bytes 3145736 | tf_op jit(solution)/shard_map/ppermute | solution.py:510
  6.9 0.8 copy.12
  7.7 0.1 broadcast_in_dim.7
  7.8 0.0 copy-start.6
  7.8 0.7 copy-done.6
  8.4 0.0 copy-start.7
  8.4 0.7 copy-done.7
  9.1 0.0 copy-start.1
  9.1 0.0 copy-start.2
  9.1 0.0 copy-start.5
  9.1 7.8 %assemble.1.dense = bf16[2048,2048]{1,0:T(8,128)(2,1)S(1)} custom-call(s32[128]{0:T(128)S(1)} %bitcast.11, s32[128]{0:T(128)S(1)} %bitcast.12, s32[1]{0:T(128)} %bitcast.8.count, f32[128,128,128]{2,1,0:T(8,128)} %bitcast.13), custom_call_target="tpu_custom_call" | custom-call | bytes 33554432 | tf_op jit(solution)/shard_map/assemble/pallas_call | solution.py:41
  16.9 0.0 copy-start
  16.9 3.2 %copy-done = bf16[2048,2048]{1,0:T(8,128)(2,1)} copy-done((bf16[2048,2048]{1,0:T(8,128)(2,1)}, bf16[2048,2048]{1,0:T(8,128)(2,1)S(1)}, u32[]{:S(2)}) %copy-start) | copy-done | bytes 8388632
  20.2 7.5 %collective-permute-done.from_left = f32[512,512]{1,0:T(8,128)S(1)} collective-permute-done((f32[512,512]{1,0:T(8,128)}, f32[512,512]{1,0:T(8,128)S(1)}, u32[]{:S(2)}, u32[]{:S(2)}) %collective-permute-start) | collective-permute-done | bytes 1048608 | tf_op jit(solution)/shard_map/ppermute | solution.py:509
  27.6 4.1 %collective-permute-done.1.from_right = f32[512,512]{1,0:T(8,128)S(1)} collective-permute-done((f32[512,512]{1,0:T(8,128)}, f32[512,512]{1,0:T(8,128)S(1)}, u32[]{:S(2)}, u32[]{:S(2)}) %collective-permute-start.1) | collective-permute-done | bytes 1048608 | tf_op jit(solution)/shard_map/ppermute | solution.py:510
  31.7 0.1 broadcast_in_dim.8.wanted
  31.8 0.0 copy-done.1
  31.8 0.0 copy-done.2
  31.8 0.0 copy-done.3
  31.8 0.0 copy-done.4
  31.8 0.0 copy-done.5
  31.8 76.3 %layer.1 = bf16[512,512]{1,0:T(8,128)(2,1)S(1)} custom-call(f32[512,512]{1,0:T(8,128)S(1)} %copy-done.3, f32[512,512]{1,0:T(8,128)S(1)} %collective-permute-done.from_left, f32[512,512]{1,0:T(8,128)S(1)} %collective-permute-done.1.from_right, s32[16,128]{1,0:T(8,128)S(1)} %broadcast_in_dim.8.wanted, bf16[2048,2048]{1,0:T(8,128)(2,1)} %copy-done, ...), custom_call_target="tpu_custom_call" | custom-call | tf_op jit(solution)/shard_map/layer/pallas_call | solution.py:461
  108.2 0.8 copy.15
  (2 shorter events, 0.0 us)
Async XLA Ops:
  0.0 27.6 %collective-permute-start = (f32[512,512]{1,0:T(8,128)}, f32[512,512]{1,0:T(8,128)S(1)}, u32[]{:S(2)}, u32[]{:S(2)}) collective-permute-start(f32[512,512]{1,0:T(8,128)} %features.1), channel_id=1, source_target_pairs={{0,8},{4,12},{8,16},{12,20},{16,24},{20,28},{1,9},{5,13},{9,17},{1... | collective-permute-start | bytes 3145736 | tf_op jit(solution)/shard_map/ppermute | solution.py:509
  5.0 26.7 %collective-permute-start.1 = (f32[512,512]{1,0:T(8,128)}, f32[512,512]{1,0:T(8,128)S(1)}, u32[]{:S(2)}, u32[]{:S(2)}) collective-permute-start(f32[512,512]{1,0:T(8,128)} %features.1), channel_id=1, source_target_pairs={{8,0},{12,4},{16,8},{20,12},{24,16},{28,20},{9,1},{13,5},{17,9},{2... | collective-permute-start | bytes 3145736 | tf_op jit(solution)/shard_map/ppermute | solution.py:510
  7.8 0.7 copy-start.6
  8.4 0.7 copy-start.7
  9.1 22.7 %copy-start.1 = (bf16[512,2048]{1,0:T(8,128)(2,1)S(1)}, bf16[512,2048]{1,0:T(8,128)(2,1)}, u32[]{:S(2)}) copy-start(bf16[512,2048]{1,0:T(8,128)(2,1)} %w_in.1) | copy-start | bytes 6291460
  9.1 22.7 %copy-start.2 = (bf16[2048,512]{1,0:T(8,128)(2,1)S(1)}, bf16[2048,512]{1,0:T(8,128)(2,1)}, u32[]{:S(2)}) copy-start(bf16[2048,512]{1,0:T(8,128)(2,1)} %w_out.1) | copy-start | bytes 6291460
  9.1 22.7 %copy-start.3 = (f32[512,512]{1,0:T(8,128)S(1)}, f32[512,512]{1,0:T(8,128)}, u32[]{:S(2)}) copy-start(f32[512,512]{1,0:T(8,128)} %features.1) | copy-start | bytes 3145732
  9.1 22.7 %copy-start.4 = (f32[2048]{0:T(1024)S(1)}, f32[2048]{0:T(1024)}, u32[]{:S(2)}) copy-start(f32[2048]{0:T(1024)} %param.17) | copy-start | bytes 24580
  9.1 22.7 %copy-start.5 = (f32[512]{0:T(512)S(1)}, f32[512]{0:T(512)}, u32[]{:S(2)}) copy-start(f32[512]{0:T(512)} %param.19) | copy-start | bytes 6148
  16.9 3.2 %copy-start = (bf16[2048,2048]{1,0:T(8,128)(2,1)}, bf16[2048,2048]{1,0:T(8,128)(2,1)S(1)}, u32[]{:S(2)}) copy-start(bf16[2048,2048]{1,0:T(8,128)(2,1)S(1)} %assemble.1.dense) | copy-start | bytes 25165828
